TPU v7x, 32 devices: a whole 2x2x4 slice. The times are simulated.
32 devices in a mesh: member: 8 (over y, x, core), space: 4 (over z).
Axes of the slice: x: 2, y: 2, z: 4, core: 2. Of those that a mesh axis runs over, the one named last changes fastest.
Arguments:
- background: bfloat16 [256, 4, 16384], P('member', None, 'space'), may hold values from -6 to 6
- obs_ens: float32 [256, 32768], P('member', 'space'), may hold values from -6 to 6
- observed: float32 [32768], P('space'), may hold values from -8 to 8
- variance: float32 [32768], P('space'), may hold values from 0.5 to 4
- obs_slot: int32 [4, 16, 512], P('space', 'member'), may hold values from 0 to 24575
- obs_count: int32 [4, 16], P('space', 'member'), may hold values from 256 to 512
- loc_bin: int32 [4, 16, 512], P('space', 'member'), may hold values from 0 to 31
Outputs:
- analysis: bfloat16 [256, 4, 16384], P('member', None, 'space')
All inputs are finite; a program needn't handle non-finite values.
Results may differ from a plain program's by a relative error of at most 0.0056.
Values may be sent and summed in bfloat16 or wider, within the bound.
A program may use at most 192 MiB of HBM per device.

v0:
```python
import jax
import jax.numpy as jnp
from jax import lax
from jax.sharding import PartitionSpec as P

ITERS = 8
NBINS = 32


def padded(x, sides, width):
    for axis, dim in sides:
        devices, length = (lax.axis_size(axis), x.shape[dim])
        up = [(i, (i + 1) % devices) for i in range(devices)]
        down = [(j, i) for i, j in up]
        last = lax.slice_in_dim(x, length - width, length, axis=dim)
        leading = lax.slice_in_dim(x, 0, width, axis=dim)
        before = lax.ppermute(last, axis, up)
        after = lax.ppermute(leading, axis, down)
        x = jnp.concatenate([before, x, after], axis=dim)
    return x


def localize(bin_idx):
    scaled = bin_idx.astype(jnp.float32) / (NBINS * 0.375)
    return jnp.exp(-0.5 * scaled * scaled)


def transforms(columns, departure, weight):
    members = columns.shape[0]
    highest = lax.Precision.HIGHEST
    scaled = columns * weight[None]
    gram_mat = jnp.einsum("kbp,jbp->bkj", scaled, columns, precision=highest)
    identity = jnp.eye(members, dtype=jnp.float32)
    system = gram_mat + (members - 1.0) * identity[None]
    half_trace = 0.5 * jnp.trace(system, axis1=1, axis2=2)
    root_iter = system / half_trace[:, None, None]
    inv_root = jnp.broadcast_to(identity[None], root_iter.shape)
    for sweep_num in range(ITERS):
        correct = 1.5 * identity[None] - 0.5 * jnp.einsum(
            "bij,bjk->bik", inv_root, root_iter, precision=highest
        )
        root_iter = jnp.einsum("bij,bjk->bik", root_iter, correct, precision=highest)
        inv_root = jnp.einsum("bij,bjk->bik", correct, inv_root, precision=highest)
    covariance = (
        jnp.einsum("bij,bjk->bik", inv_root, inv_root, precision=highest)
        / half_trace[:, None, None]
    )
    pulled = jnp.einsum("kbp,bp->bk", scaled, departure, precision=highest)
    mean_shift = jnp.einsum("bij,bj->bi", covariance, pulled, precision=highest)
    spread = inv_root * jnp.sqrt((members - 1.0) / half_trace)[:, None, None]
    return (spread + mean_shift[:, :, None]).astype(jnp.bfloat16)


def analyse(columns, weights_tot):
    members, levels, span_cols = columns.shape
    blocks = weights_tot.shape[0]
    average = jnp.mean(columns.astype(jnp.float32), axis=0)
    perturb = (columns.astype(jnp.float32) - average[None]).astype(jnp.bfloat16)
    blocked = perturb.reshape(members, levels, blocks, span_cols // blocks)
    increment = jnp.einsum(
        "klbc,bkn->nlbc", blocked, weights_tot, preferred_element_type=jnp.float32
    )
    return (increment.reshape(members, levels, span_cols) + average[None]).astype(jnp.bfloat16)


def per_device(background, obs_ens, observed, variance, obs_slot, obs_count, loc_bin):
    tile_obs = observed.shape[0]
    slot_idx = obs_slot[0]
    member_total = lax.axis_size("member")
    own_rows = obs_ens.shape[0]
    all_rows = own_rows * member_total
    obs_mean = (
        lax.psum(jnp.sum(obs_ens, axis=0).astype(jnp.bfloat16), "member").astype(jnp.float32)
        / all_rows
    )
    own_pert = obs_ens - obs_mean[None]
    joined = jnp.concatenate([own_pert, (observed - obs_mean)[None], variance[None]], axis=0)
    nearby = padded(joined, (("space", 1),), tile_obs)
    every_slot = lax.all_gather(obs_slot, "member", axis=1, tiled=True)
    picked = jnp.take(nearby[:-2], every_slot[0], axis=1)
    columns = lax.all_to_all(picked, "member", split_axis=1, concat_axis=0, tiled=True)
    side_cols = jnp.take(nearby[-2:], slot_idx, axis=1)
    dep_cols = side_cols[0]
    var_cols = side_cols[1]
    in_range = jnp.arange(slot_idx.shape[1], dtype=jnp.int32)[None, :] < obs_count[0][:, None]
    weight = jnp.where(in_range, localize(loc_bin[0]) / var_cols, 0.0)
    weights_tot = transforms(columns, dep_cols, weight)
    gathered = lax.all_to_all(background, "member", split_axis=2, concat_axis=0, tiled=True)
    result = lax.all_to_all(
        analyse(gathered, weights_tot), "member", split_axis=0, concat_axis=2, tiled=True
    )
    return result


def solution(mesh):
    in_specs = (
        P("member", None, "space"),
        P("member", "space"),
        P("space"),
        P("space"),
        P("space", "member", None),
        P("space", "member"),
        P("space", "member", None),
    )
    out_specs = P("member", None, "space")
    return jax.shard_map(
        per_device, mesh=mesh, in_specs=in_specs, out_specs=out_specs, check_vma=False
    )
```

profile of v0, /device:TPU:1, one launch (start us, length us, event | category | flops | bytes accessed | tf_op | source)
XLA Modules:
  0.0 206.7 jit_solution(6720403337312078480)
XLA Ops:
  0.0 1.3 reduce_sum.35
  1.3 22.4 %psum.7 = bf16[8192]{0:T(1024)(128)(2,1)S(1)} all-reduce(bf16[8192]{0:T(1024)(128)(2,1)S(1)} %reduce_sum.35), channel_id=1, replica_groups=mesh['member'=8,'space'=4] {'member'}, use_global_device_ids=true, to_apply=%region_1.0 | all-reduce | flops 8192 | bytes 32768 | tf_op jit(solution)/shard_map/psum | solution.py:73
  23.7 0.8 convert_multiply_fusion
  24.5 1.4 broadcast_subtract_fusion
  25.9 1.2 pad_maximum_fusion.1
  27.1 3.3 %collective-permute-start.1 = (f32[34,8192]{1,0:T(8,128)}, f32[34,8192]{1,0:T(8,128)}, u32[]{:S(2)}, u32[]{:S(2)}) collective-permute-start(f32[34,8192]{1,0:T(8,128)} %pad_maximum_fusion.1), channel_id=1, source_target_pairs={{1,0},{2,1},{3,2},{0,3},{5,4},{6,5},{7,6},{4,7},{9,8},{10,9},{11,1... | collective-permute-start | bytes 3342344 | tf_op jit(solution)/shard_map/ppermute | solution.py:18
  30.4 4.8 %copy.67 = bf16[32,4,4096]{0,1,2:T(4,128)(2,1)} copy(bf16[32,4,4096]{2,1,0:T(4,128)(2,1)S(1)} %copy-done) | data formatting | bytes 2097152 | tf_op args[0]
  35.2 7.8 %reshape.178 = bf16[8,2,32768]{2,1,0:T(2,128)(2,1)} reshape(bf16[4096,4,32]{2,1,0:T(4,128)(2,1)} %bitcast.115) | data formatting | bytes 2097152
  43.0 7.1 %all-to-all-start.1 = ((bf16[8,2,32768]{2,1,0:T(2,128)(2,1)}), bf16[8,2,32768]{2,1,0:T(2,128)(2,1)S(1)}, u32[]{:S(2)}, u32[]{:S(2)}) async-start(bf16[8,2,32768]{2,1,0:T(2,128)(2,1)} %reshape.178), calls=%async_computation.1 | async-start | bytes 2097152 | tf_op jit(solution)/shard_map/all_to_all | solution.py:88
  51.3 0.7 fusion.27
  52.1 16.5 %all_gather.3 = s32[1,16,512]{2,0,1:T(1,128)S(1)} all-gather(s32[1,2,512]{2,0,1:T(1,128)S(1)} %copy.61), channel_id=1, replica_groups=mesh['member'=8,'space'=4] {'member'}, dimensions={1}, use_global_device_ids=true | all-gather | bytes 36864 | tf_op jit(solution)/shard_map/all_gather | solution.py:79
  69.3 0.7 fusion.26
  70.0 4.5 %reshape.179 = bf16[4096,4,32]{2,1,0:T(4,128)(2,1)} reshape(bf16[8,2,32768]{2,1,0:T(2,128)(2,1)S(1)} %all-to-all-done.1) | data formatting | bytes 2097152
  74.5 6.0 %copy.68 = f32[32,4,8,512]{3,0,2,1:T(8,128)S(1)} copy(bf16[32,4,8,512]{0,1,3,2:T(4,128)(2,1)} %bitcast.114) | data formatting | bytes 3145728 | tf_op jit(solution)/shard_map/convert_element_type | solution.py:58
  80.5 2.4 %reshape.152 = f32[256,4,2,256]{3,2,0,1:T(2,128)} reshape(f32[8,32,4,512]{3,1,0,2:T(8,128)S(1)} %bitcast.119) | data formatting | bytes 4194304 | tf_op jit(solution)/shard_map/convert_element_type | solution.py:58
  82.9 8.1 %convert_reduce_fusion = f32[4,4096]{0,1:T(8,128)S(1)} fusion(bf16[4096,4,32]{2,1,0:T(4,128)(2,1)} %reshape.179), kind=kLoop, calls=%fused_computation.5 | loop fusion | flops 1032192 | bytes 1114112 | tf_op jit(solution)/shard_map/reduce_sum | solution.py:57
  91.0 0.9 reduce_sum.39
  91.9 1.0 broadcast_multiply_fusion
  93.1 2.3 %subtract_convert_fusion = bf16[256,4,2,256]{3,2,0,1:T(2,128)(2,1)S(1)} fusion(f32[256,4,2,256]{3,2,0,1:T(2,128)} %reshape.152, f32[4,2,256]{2,1,0:T(2,128)S(1)} %copy.70), kind=kLoop, calls=%fused_computation.6 | loop fusion | flops 1048576 | bytes 3153920 | tf_op jit(solution)/shard_map/convert_element_type | solution.py:58
  95.4 2.0 pad_maximum_fusion
  97.4 1.8 slice.20
  99.3 8.4 %copy.87 = f32[32,24576]{0,1:T(8,128)} copy(f32[32,24576]{1,0:T(8,128)} %slice.20) | data formatting | bytes 6291456
  107.6 32.3 %gather_fusion = f32[8192,32]{1,0:T(8,128)} fusion(f32[32,24576]{0,1:T(8,128)} %copy.87, s32[8192]{0:T(1024)S(1)} %copy-done.4), kind=kCustom, calls=%fused_computation | custom fusion | bytes 2129920 | tf_op jit(solution)/shard_map/jit(_take)/gather | solution.py:80
  140.0 2.8 %copy.63 = f32[16,512,32]{1,2,0:T(8,128)S(1)} copy(f32[16,512,32]{2,1,0:T(8,128)} %bitcast.120) | data formatting | bytes 2097152 | tf_op jit(solution)/shard_map/jit(_take)/gather | solution.py:80
  142.8 1.2 select_bitcast_fusion
  143.9 3.6 %all-to-all-start = ((f32[32,16,512]{2,0,1:T(8,128)}), f32[32,16,512]{2,0,1:T(8,128)S(1)}, u32[]{:S(2)}, u32[]{:S(2)}) async-start(f32[32,16,512]{2,0,1:T(8,128)} %select_bitcast_fusion), calls=%async_computation | async-start | bytes 2097152 | tf_op jit(solution)/shard_map/all_to_all | solution.py:81
  147.6 1.8 pad_maximum_fusion.2
  149.4 7.5 %copy.65 = f32[2,24576]{0,1:T(8,128)} copy(f32[2,24576]{1,0:T(2,128)} %pad_maximum_fusion.2) | data formatting | bytes 393216 | tf_op jit(solution)/shard_map/slice | solution.py:82
  156.9 7.6 %gather_fusion.1 = f32[1024,2]{1,0:T(8,128)S(1)} fusion(f32[2,24576]{0,1:T(8,128)} %copy.65, s32[1024]{0:T(1024)S(1)} %copy-done.6), kind=kCustom, calls=%fused_computation.1 | custom fusion | bytes 20480 | tf_op jit(solution)/shard_map/jit(_take)/gather | solution.py:82
  164.9 1.3 select_reduce_fusion
  166.2 0.7 fusion.15
  167.0 0.7 fusion.29
  168.3 0.7 fusion.14
  170.3 0.7 fusion.13
  170.9 0.7 fusion.39
  172.3 0.7 fusion.12
  174.2 0.7 fusion.11
  175.6 0.7 fusion.42
  176.2 0.7 fusion.10
  176.9 0.9 fusion.45
  178.5 0.7 fusion.9
  180.4 1.0 fusion.1
  181.5 0.7 fusion.8
  182.8 0.7 convolution_divide_fusion
  184.0 0.7 convolution_bitcast_fusion
  185.2 1.0 copy.74
  186.2 18.1 %all_to_all.45 = bf16[256,4,512]{2,1,0:T(4,128)(2,1)S(1)} all-to-all(bf16[256,4,512]{2,1,0:T(4,128)(2,1)S(1)} %copy.74), channel_id=1, replica_groups=mesh['member'=8,'space'=4] {'member'}, dimensions={0} | all-to-all | bytes 2097152 | tf_op jit(solution)/shard_map/all_to_all | solution.py:89
  205.1 1.6 reshape.177
  (60 shorter events, 11.5 us)
Async XLA Ops:
  0.0 25.9 %copy-start.3 = (f32[8192]{0:T(1024)S(1)}, f32[8192]{0:T(1024)}, u32[]{:S(2)}) copy-start(f32[8192]{0:T(1024)} %param.10) | copy-start | bytes 98308
  24.5 5.9 %copy-start = (bf16[32,4,4096]{2,1,0:T(4,128)(2,1)S(1)}, bf16[32,4,4096]{2,1,0:T(4,128)(2,1)}, u32[]{:S(2)}) copy-start(bf16[32,4,4096]{2,1,0:T(4,128)(2,1)} %param.7) | copy-start | bytes 3145732
  27.1 68.3 %collective-permute-start.1 = (f32[34,8192]{1,0:T(8,128)}, f32[34,8192]{1,0:T(8,128)}, u32[]{:S(2)}, u32[]{:S(2)}) collective-permute-start(f32[34,8192]{1,0:T(8,128)} %pad_maximum_fusion.1), channel_id=1, source_target_pairs={{1,0},{2,1},{3,2},{0,3},{5,4},{6,5},{7,6},{4,7},{9,8},{10,9},{11,1... | collective-permute-start | bytes 3342344 | tf_op jit(solution)/shard_map/ppermute | solution.py:18
  30.4 65.0 %collective-permute-start = (f32[34,8192]{1,0:T(8,128)}, f32[34,8192]{1,0:T(8,128)}, u32[]{:S(2)}, u32[]{:S(2)}) collective-permute-start(f32[34,8192]{1,0:T(8,128)} %pad_maximum_fusion.1), channel_id=1, source_target_pairs={{0,1},{1,2},{2,3},{3,0},{4,5},{5,6},{6,7},{7,4},{8,9},{9,10},{10,1... | collective-permute-start | bytes 3342344 | tf_op jit(solution)/shard_map/ppermute | solution.py:17
  43.0 7.1 %copy-start.5 = (s32[1,2,512]{2,1,0:T(2,128)S(1)}, s32[1,2,512]{2,1,0:T(2,128)}, u32[]{:S(2)}) copy-start(s32[1,2,512]{2,1,0:T(2,128)} %param.11) | copy-start | bytes 12292
  43.0 27.0 %all-to-all-start.1 = ((bf16[8,2,32768]{2,1,0:T(2,128)(2,1)}), bf16[8,2,32768]{2,1,0:T(2,128)(2,1)S(1)}, u32[]{:S(2)}, u32[]{:S(2)}) async-start(bf16[8,2,32768]{2,1,0:T(2,128)(2,1)} %reshape.178), calls=%async_computation.1 | async-start | bytes 2097152 | tf_op jit(solution)/shard_map/all_to_all | solution.py:88
  99.3 8.4 %copy-start.4 = (s32[8192]{0:T(1024)S(1)}, s32[8192]{0:T(1024)}, u32[]{:S(2)}) copy-start(s32[8192]{0:T(1024)} %broadcast_clamp_fusion) | copy-start | bytes 98308
  143.9 20.9 %all-to-all-start = ((f32[32,16,512]{2,0,1:T(8,128)}), f32[32,16,512]{2,0,1:T(8,128)S(1)}, u32[]{:S(2)}, u32[]{:S(2)}) async-start(f32[32,16,512]{2,0,1:T(8,128)} %select_bitcast_fusion), calls=%async_computation | async-start | bytes 2097152 | tf_op jit(solution)/shard_map/all_to_all | solution.py:81
  149.4 7.5 %copy-start.6 = (s32[1024]{0:T(1024)S(1)}, s32[1024]{0:T(1024)}, u32[]{:S(2)}) copy-start(s32[1024]{0:T(1024)} %broadcast_clamp_fusion.1) | copy-start | bytes 12292
  149.4 15.3 %copy-start.7 = (pred[2,512]{1,0:T(4,128)(4,1)S(1)}, pred[2,512]{1,0:T(4,128)(4,1)}, u32[]{:S(2)}) copy-start(pred[2,512]{1,0:T(4,128)(4,1)} %compare_and_fusion.1) | copy-start | bytes 3076
  149.4 15.3 %copy-start.8 = (s32[1,2,512]{2,1,0:T(2,128)S(1)}, s32[1,2,512]{2,1,0:T(2,128)}, u32[]{:S(2)}) copy-start(s32[1,2,512]{2,1,0:T(2,128)} %param.13) | copy-start | bytes 12292
  149.4 15.3 %copy-start.9 = (s32[1,2]{1,0:T(1,128)S(1)}, s32[1,2]{1,0:T(1,128)}, u32[]{:S(2)}) copy-start(s32[1,2]{1,0:T(1,128)} %param.12) | copy-start | bytes 28
  156.9 8.0 %copy-start.2 = (f32[256,256]{1,0:T(8,128)S(1)}, f32[256,256]{1,0:T(8,128)}, u32[]{:S(2)}) copy-start(f32[256,256]{1,0:T(8,128)} %fusion.26) | copy-start | bytes 786436
  164.8 1.4 copy-start.1
where the time goes:
time: 209 us; the launch traced here: 207 us
  local copies, waits for them, and re-layouts  90 us (43%)
  blocking collectives  57 us (27%)
  other arithmetic  25.7 us (12%)
  matrix products  19.6 us (9%)
  starting transfers between devices  14.1 us (7%)
    gather x2, local copies, waits for them, and re-layouts, per_device(): picked = jnp.take(nearby[:-2], every_slot[0], axis=1)  35.1 us
    unnamed x26, local copies, waits for them, and re-layouts  25.5 us
    psum x1, blocking collectives, per_device(): lax.psum(jnp.sum(obs_ens, axis=0).astype(jnp.bfloat16), 'member')  22.4 us
    all_to_all x1, blocking collectives, per_device(): lax.all_to_all(analyse(gathered, weights_tot), 'member', split_axis=0, co...  18.1 us
    all_gather x1, blocking collectives, per_device(): every_slot = lax.all_gather(obs_slot, 'member', axis=1, tiled=True)  16.5 us
    reduce_sum x2, other arithmetic, analyse(): average = jnp.mean(columns.astype(jnp.float32), axis=0)  9 us
    convert_element_type x2, local copies, waits for them, and re-layouts, analyse(): perturb = (columns.astype(jnp.float32) - average[None]).astype(jnp.bfloat16)  8.38 us
    gather x2, local copies, waits for them, and re-layouts, per_device(): side_cols = jnp.take(nearby[-2:], slot_idx, axis=1)  7.78 us
  transfers between devices with their start and end apart: 4, of which 0 were waited for; matrix products, arithmetic and copies ran while one was open for 28% of the time, Pallas kernels for 0%

commit v1 on v0

v1 whole, which is shorter than its diff:
```python
import jax
import jax.numpy as jnp
from jax import lax
from jax.experimental import pallas as pl
from jax.experimental.pallas import tpu as pltpu
from jax.sharding import PartitionSpec as P

ITERS = 8
NBINS = 32
F32 = jnp.float32
BF16 = jnp.bfloat16


def pick_kernel(slot_ref, before_ref, own_ref, after_ref, sbefore_ref, sown_ref, safter_ref,
                out_ref, side_ref, table, rows):
    members, tile_obs = own_ref.shape
    blocks, _, slots = out_ref.shape
    for k, (src, side) in enumerate(((before_ref, sbefore_ref), (own_ref, sown_ref), (after_ref, safter_ref))):
        @pl.loop(0, tile_obs // 512)
        def _(c, k=k, src=src, side=side):
            for u in range(4):
                at = pl.multiple_of(c * 512 + u * 128, 128)
                x = jnp.concatenate(
                    [src[:, pl.ds(at, 128)].astype(F32), side[:, pl.ds(at, 128)],
                     jnp.zeros((128 - members - 8, 128), F32)], axis=0)
                table[pl.ds(pl.multiple_of(k * tile_obs + at, 128), 128), :] = x.T

    @pl.loop(0, blocks)
    def _(b):
        @pl.loop(0, slots // 32)
        def _(g):
            base = pl.multiple_of(g * 32, 32)
            for u in range(32):
                i = slot_ref[b * slots + base + u]
                rows[pl.ds(base + u, 1), :] = table[pl.ds(i, 1), :]
        for u in range(slots // 128):
            t = rows[u * 128:(u + 1) * 128, :].T
            out_ref[b, :, u * 128:(u + 1) * 128] = t[:members].astype(BF16)
            side_ref[b, :, u * 128:(u + 1) * 128] = t[members:members + 8]


def pick(slots, tables, sides, blocks, width):
    members, tile_obs = tables[0].shape
    vmem = pl.BlockSpec(memory_space=pltpu.VMEM)
    return pl.pallas_call(
        pick_kernel,
        out_shape=(jax.ShapeDtypeStruct((blocks, members, width), BF16),
                   jax.ShapeDtypeStruct((blocks, 8, width), F32)),
        in_specs=[pl.BlockSpec(memory_space=pltpu.SMEM)] + [vmem] * 6,
        out_specs=(vmem, vmem),
        scratch_shapes=[pltpu.VMEM((3 * tile_obs, 128), F32), pltpu.VMEM((width, 128), F32)],
        compiler_params=pltpu.CompilerParams(vmem_limit_bytes=50 * 2**20),
        name="pick",
    )(slots, *tables, *sides)


def dot1(a, b, nt=False):
    dims = (((1,), (1 if nt else 0,)), ((), ()))
    return lax.dot_general(a.astype(BF16), b.astype(BF16), dims, preferred_element_type=F32)


def dot3(a, b):
    ah, bh = a.astype(BF16), b.astype(BF16)
    al, bl = (a - ah.astype(F32)).astype(BF16), (b - bh.astype(F32)).astype(BF16)
    return dot1(ah, bh) + (dot1(ah, bl) + dot1(al, bh))


def eye(n):
    return (lax.broadcasted_iota(jnp.int32, (n, n), 0) == lax.broadcasted_iota(jnp.int32, (n, n), 1)).astype(F32)


def roots(x, observed, variance, loc_bin, count):
    members, slots = x[0].shape
    ident = eye(members)
    ys, zs, halves, pulls = [], [], [], []
    for b in range(len(x)):
        mean = jnp.sum(x[b], axis=0, keepdims=True) * (1.0 / members)
        pert = x[b] - mean
        scaled = loc_bin[b].astype(F32) / (NBINS * 0.375)
        weight = jnp.exp(-0.5 * scaled * scaled) / variance[b]
        weight = jnp.where(lax.broadcasted_iota(jnp.int32, (1, slots), 1) < count[b], weight, 0.0)
        root_w = pert * jnp.sqrt(weight)
        gram = dot1(root_w, root_w, nt=True)
        system = gram + (members - 1.0) * ident
        half = 0.5 * jnp.sum(system * ident)
        pulls.append(jnp.sum(pert * (weight * (observed[b] - mean)), axis=1, keepdims=True))
        halves.append(half)
        ys.append(system / half)
        zs.append(None)
    for sweep in range(ITERS):
        for b in range(len(x)):
            y, z = ys[b], zs[b]
            if z is None:
                m = y
                zs[b] = 1.5 * ident - 0.5 * m
                ys[b] = 1.5 * y - 0.5 * dot1(y, m)
                continue
            m = dot1(z, y) if sweep < ITERS - 2 else dot3(z, y)
            if sweep < ITERS - 3:
                zs[b] = 1.5 * z - 0.5 * dot1(m, z)
                ys[b] = 1.5 * y - 0.5 * dot1(y, m)
            else:
                e = ident - m
                zs[b] = z + 0.5 * dot1(e, z)
                if sweep < ITERS - 1:
                    ys[b] = y + 0.5 * dot1(y, e)
    return zs, halves, pulls


def weights_t(z, half, pulled):
    members = z.shape[0]
    ident = eye(members)
    inner = jnp.sum(z * pulled, axis=0, keepdims=True)
    shift = jnp.sum(z * inner, axis=1, keepdims=True) / half
    shift_row = jnp.sum(shift * ident, axis=0, keepdims=True)
    return (jnp.sqrt((members - 1.0) / half) * z + shift_row).astype(BF16)


def spread_levels(wt, levels):
    members = wt.shape[0]
    n = members * levels
    r0 = lax.broadcasted_iota(jnp.int32, (n, members), 0) // levels
    up = (r0 == lax.broadcasted_iota(jnp.int32, (n, members), 1)).astype(BF16)
    tall = dot1(up, wt)
    wide = dot1(tall, up, nt=True)
    same = (lax.broadcasted_iota(jnp.int32, (n, n), 0) % levels) == (lax.broadcasted_iota(jnp.int32, (n, n), 1) % levels)
    return jnp.where(same, wide, 0.0).astype(BF16)


def analyse(f, w4, levels):
    n, cols = f.shape
    members = n // levels
    f = f.astype(F32).reshape(n // 8, 8, cols)
    total = jnp.sum(f, axis=0)
    step = levels
    while step < 8:
        total = total + pltpu.roll(total, step, 0)
        step *= 2
    mean = total * (1.0 / members)
    pert = (f - mean[None]).reshape(n, cols)
    inc = dot1(w4, pert)
    return (inc.reshape(n // 8, 8, cols) + mean[None]).reshape(n, cols).astype(BF16)


def main_kernel(count_ref, levels, picks_ref, side_ref, bin_ref, field_ref, out_ref):
    parts, blocks, share, slots = picks_ref.shape
    members = parts * share
    rows, cols = field_ref.shape[0] * field_ref.shape[1], field_ref.shape[2]
    cut = cols // blocks
    x = [picks_ref[:, b].reshape(members, slots).astype(F32) for b in range(blocks)]
    zs, halves, pulls = roots(
        x, [side_ref[b, 0:1] for b in range(blocks)], [side_ref[b, 1:2] for b in range(blocks)],
        [bin_ref[b:b + 1] for b in range(blocks)], [count_ref[b] for b in range(blocks)])
    for b in range(blocks):
        w4 = spread_levels(weights_t(zs[b], halves[b], pulls[b]), levels)
        f = field_ref[:, :, b * cut:(b + 1) * cut].reshape(rows, cut)
        out_ref[:, :, b * cut:(b + 1) * cut] = analyse(f, w4, levels).reshape(parts, rows // parts, cut)


def per_device(background, obs_ens, observed, variance, obs_slot, obs_count, loc_bin):
    devices = lax.axis_size("member")
    space = lax.axis_size("space")
    share, levels, columns = background.shape
    blocks, width = obs_slot.shape[1:]
    up = [(i, (i + 1) % space) for i in range(space)]
    down = [(j, i) for i, j in up]
    own = obs_ens.astype(BF16)
    side = jnp.concatenate([observed[None], variance[None], jnp.zeros((6, observed.shape[0]), F32)], axis=0)
    tables = (lax.ppermute(own, "space", up), own, lax.ppermute(own, "space", down))
    short = side[:2]
    grow = lambda s: jnp.concatenate([s, jnp.zeros((6, s.shape[1]), F32)], axis=0)
    sides = (grow(lax.ppermute(short, "space", up)), side, grow(lax.ppermute(short, "space", down)))
    every_slot = lax.all_gather(obs_slot[0], "member", axis=0, tiled=True).reshape(-1)
    picked, picked_side = pick(every_slot, tables, sides, devices * blocks, width)
    picked = picked.reshape(devices, blocks, share, width)
    picks = lax.all_to_all(picked, "member", split_axis=0, concat_axis=0, tiled=True)
    mine = lax.dynamic_slice_in_dim(picked_side, lax.axis_index("member") * blocks, blocks, 0)
    flat = background.reshape(share * levels, devices, columns // devices).transpose(1, 0, 2)
    fields = lax.all_to_all(flat, "member", split_axis=0, concat_axis=0, tiled=True)
    vmem = pl.BlockSpec(memory_space=pltpu.VMEM)
    out = pl.pallas_call(
        lambda c, *refs: main_kernel(c, levels, *refs),
        out_shape=jax.ShapeDtypeStruct(fields.shape, BF16),
        in_specs=[pl.BlockSpec(memory_space=pltpu.SMEM)] + [vmem] * 4,
        out_specs=vmem,
        compiler_params=pltpu.CompilerParams(vmem_limit_bytes=50 * 2**20),
        name="analysis",
    )(obs_count[0], picks, mine, loc_bin[0], fields)
    back = lax.all_to_all(out, "member", split_axis=0, concat_axis=0, tiled=True)
    return back.transpose(1, 0, 2).reshape(share, levels, columns)


def solution(mesh):
    in_specs = (
        P("member", None, "space"), P("member", "space"), P("space"), P("space"),
        P("space", "member", None), P("space", "member"), P("space", "member", None),
    )
    return jax.shard_map(per_device, mesh=mesh, in_specs=in_specs,
                         out_specs=P("member", None, "space"), check_vma=False)
```

time: 209 us -> 96.6 us (0.46)
  local copies, waits for them, and re-layouts: 90 us -> 6.64 us
  Pallas kernels: 0 us -> 25.2 us
  other arithmetic: 25.7 us -> 2.2 us
  blocking collectives: 57 us -> 37.2 us
  matrix products: 19.6 us -> 0 us
  waiting for transfers between devices: 0.01 us -> 6.76 us
  starting transfers between devices: 14.1 us -> 16.7 us
    gather x4 -> x0, local copies, waits for them, and re-layouts: 42.9 us -> none  [the longest x2 35.1 us: per_device(): picked = jnp.take(nearby[:-2], every_slot[0], axis=1)]
    pallas_call x0 -> x2, Pallas kernels: none -> 25.2 us  [the longest x1 17.8 us: pick(): pl.pallas_call(pick_kernel, out_shape=(jax.ShapeDtypeStruct((blocks, memb...]
    unnamed x26 -> x11, local copies, waits for them, and re-layouts: 25.5 us -> 1.26 us
    psum x1 -> x0, blocking collectives: 22.4 us -> none  [per_device(): lax.psum(jnp.sum(obs_ens, axis=0).astype(jnp.bfloat16), 'member')]
    dot_general x28 -> x0, matrix products: 19.6 us -> none  [the longest x8 5.33 us: transforms(): jnp.einsum('bij,bjk->bik', inv_root, root_iter, precision=highest)]
    reduce_sum x3 -> x0, other arithmetic: 10.3 us -> none  [the longest x2 9 us: analyse(): average = jnp.mean(columns.astype(jnp.float32), axis=0)]
    convert_element_type x3 -> x0, local copies, waits for them, and re-layouts: 9.4 us -> none  [the longest x2 8.38 us: analyse(): perturb = (columns.astype(jnp.float32) - average[None]).astype(jnp.bfloat16)]
    slice x2 -> x0, local copies, waits for them, and re-layouts: 9.32 us -> none  [the longest x1 7.49 us: per_device(): side_cols = jnp.take(nearby[-2:], slot_idx, axis=1)]
  transfers between devices with their start and end apart: 4 -> 6, of which waited for: 0 -> 1; matrix products, arithmetic and copies ran while one was open for 28% -> 5% of each run, Pallas kernels for 0% -> 19%
where the time goes in v1:
time: 96.6 us; the launch traced here: 94.8 us
  blocking collectives  37.2 us (39%)
  Pallas kernels  25.2 us (26%)
  starting transfers between devices  16.7 us (17%)
  waiting for transfers between devices  6.76 us (7%)
  local copies, waits for them, and re-layouts  6.64 us (7%)
  other arithmetic  2.2 us (2%)
    all_to_all x1, blocking collectives, per_device(): lax.all_to_all(out, 'member', split_axis=0, concat_axis=0, tiled=True)  19.5 us
    pallas_call x1, Pallas kernels, pick(): pl.pallas_call(pick_kernel, out_shape=(jax.ShapeDtypeStruct((blocks, memb...  17.8 us
    all_gather x1, blocking collectives, per_device(): lax.all_gather(obs_slot[0], 'member', axis=0, tiled=True).reshape(-1)  17.7 us
    pallas_call x1, Pallas kernels, per_device(): pl.pallas_call(lambda c, *refs: main_kernel(c, levels, *refs), out_shape=...  7.39 us
    all_to_all x1, waiting for transfers between devices, per_device(): lax.all_to_all(picked, 'member', split_axis=0, concat_axis=0, tiled=True)  6.75 us
    all_to_all x1, starting transfers between devices, per_device(): lax.all_to_all(flat, 'member', split_axis=0, concat_axis=0, tiled=True)  5.52 us
    all_to_all x1, starting transfers between devices, per_device(): lax.all_to_all(picked, 'member', split_axis=0, concat_axis=0, tiled=True)  3.58 us
    ppermute x1, starting transfers between devices, per_device(): lax.ppermute(own, 'space', down)  3.25 us
  transfers between devices with their start and end apart: 6, of which 1 were waited for; matrix products, arithmetic and copies ran while one was open for 5% of the time, Pallas kernels for 19%

profile of v1, /device:TPU:1, one launch (start us, length us, event | category | flops | bytes accessed | tf_op | source)
XLA Modules:
  0.0 94.8 jit_solution(12043506646687531892)
XLA Ops:
  0.0 0.8 pad_maximum_fusion
  0.8 2.2 %collective-permute-start.2 = (f32[2,8192]{1,0:T(2,128)S(1)}, f32[2,8192]{1,0:T(2,128)S(1)}, u32[]{:S(2)}, u32[]{:S(2)}) collective-permute-start(f32[2,8192]{1,0:T(2,128)S(1)} %pad_maximum_fusion), channel_id=1, source_target_pairs={{0,1},{1,2},{2,3},{3,0},{4,5},{5,6},{6,7},{7,4},{8,9},{9,10},{10,1... | collective-permute-start | bytes 196616 | tf_op jit(solution)/shard_map/ppermute | solution.py:172
  3.0 2.1 %collective-permute-start.3 = (f32[2,8192]{1,0:T(2,128)S(1)}, f32[2,8192]{1,0:T(2,128)S(1)}, u32[]{:S(2)}, u32[]{:S(2)}) collective-permute-start(f32[2,8192]{1,0:T(2,128)S(1)} %pad_maximum_fusion), channel_id=1, source_target_pairs={{1,0},{2,1},{3,2},{0,3},{5,4},{6,5},{7,6},{4,7},{9,8},{10,9},{11,1... | collective-permute-start | bytes 196616 | tf_op jit(solution)/shard_map/ppermute | solution.py:172
  5.1 1.3 %convert_element_type.3.own_ref = bf16[32,8192]{1,0:T(8,128)(2,1)S(1)} convert(f32[32,8192]{1,0:T(8,128)} %param.8) | non-fusion elementwise | flops 262144 | bytes 1572864 | tf_op jit(solution)/shard_map/convert_element_type | solution.py:167
  6.4 0.1 collective-permute-start
  6.5 3.3 %collective-permute-start.1 = (bf16[32,8192]{1,0:T(8,128)(2,1)S(1)}, bf16[32,8192]{1,0:T(8,128)(2,1)S(1)}, u32[]{:S(2)}, u32[]{:S(2)}) collective-permute-start(bf16[32,8192]{1,0:T(8,128)(2,1)S(1)} %convert_element_type.3.own_ref), channel_id=1, source_target_pairs={{1,0},{2,1},{3,2},{0,3},{5,4},{6,5},{7,6},{4,7},{9,8},{10,9},{11,1... | collective-permute-start | bytes 1572872 | tf_op jit(solution)/shard_map/ppermute | solution.py:169
  9.7 1.8 %reshape.14 = bf16[128,8,512]{2,1,0:T(8,128)(2,1)S(1)} reshape(bf16[32,4,4096]{2,1,0:T(4,128)(2,1)} %param.7) | data formatting | bytes 2097152 | tf_op jit(solution)/shard_map/reshape | solution.py:178
  11.5 1.3 %copy.14 = bf16[128,8,512]{2,0,1:T(8,128)(2,1)} copy(bf16[128,8,512]{2,1,0:T(8,128)(2,1)S(1)} %reshape.14) | data formatting | bytes 2097152 | tf_op jit(solution)/shard_map/reshape | solution.py:178
  12.8 0.0 copy-start.2
  12.8 0.0 copy-start.3
  12.8 5.5 %all-to-all-start.1 = ((bf16[8,128,512]{2,1,0:T(8,128)(2,1)}), bf16[8,128,512]{2,1,0:T(8,128)(2,1)S(1)}, u32[]{:S(2)}, u32[]{:S(2)}) async-start(bf16[8,128,512]{2,1,0:T(8,128)(2,1)} %bitcast.13), calls=%async_computation.1 | async-start | bytes 2097152 | tf_op jit(solution)/shard_map/all_to_all | solution.py:179
  18.3 0.1 pad.4.clone
  18.4 0.0 copy-done.2
  18.4 0.0 copy-done.3
  18.4 0.0 copy-start.4
  18.4 0.1 maximum_maximum_fusion.sown_ref
  18.5 0.6 copy-done.4
  19.1 17.7 %all-gather = s32[1,16,512]{2,0,1:T(1,128)S(1)} all-gather(s32[1,2,512]{2,0,1:T(1,128)S(1)} %copy.10), channel_id=2, replica_groups=mesh['member'=8,'space'=4] {'member'}, dimensions={1}, use_global_device_ids=true | all-gather | bytes 36864 | tf_op jit(solution)/shard_map/all_gather | solution.py:173
  36.8 0.0 collective-permute-done.2
  36.8 0.0 collective-permute-done.3
  36.9 0.0 collective-permute-done.before_ref
  36.9 0.0 collective-permute-done.1.after_ref
  36.9 17.8 %pick.1 = (bf16[16,32,512]{2,1,0:T(8,128)(2,1)}, f32[16,8,512]{2,1,0:T(8,128)S(1)}) custom-call(s32[8192]{0:T(1024)S(1)} %bitcast.10, bf16[32,8192]{1,0:T(8,128)(2,1)S(1)} %collective-permute-done.before_ref, bf16[32,8192]{1,0:T(8,128)(2,1)S(1)} %convert_element_type.3.own_ref, bf16[32,8192]{1,0:T(8,128)(2,1)S(1)} %collective-permute-done.1.after_ref, ...), custom_call_target="tpu_custom_call" | custom-call | tf_op jit(solution)/shard_map/pick/pallas_call | solution.py:45
  54.7 0.0 all-to-all-done.1.refs_3_
  54.7 3.6 %all-to-all-start = ((bf16[8,2,32,512]{3,2,1,0:T(8,128)(2,1)}), bf16[8,2,32,512]{3,2,1,0:T(8,128)(2,1)S(1)}, u32[]{:S(2)}, u32[]{:S(2)}) async-start(bf16[8,2,32,512]{3,2,1,0:T(8,128)(2,1)} %bitcast.4), calls=%async_computation | async-start | bytes 1048576 | tf_op jit(solution)/shard_map/all_to_all | solution.py:176
  58.3 0.0 copy-start
  58.3 6.7 %all-to-all-done.refs_0_ = bf16[8,2,32,512]{3,2,1,0:T(8,128)(2,1)S(1)} async-done(((bf16[8,2,32,512]{3,2,1,0:T(8,128)(2,1)}), bf16[8,2,32,512]{3,2,1,0:T(8,128)(2,1)S(1)}, u32[]{:S(2)}, u32[]{:S(2)}) %all-to-all-start) | async-done | bytes 524320 | tf_op jit(solution)/shard_map/all_to_all | solution.py:176
  65.1 0.0 copy-start.1
  65.1 0.0 copy-done
  65.1 0.7 copy-done.1
  65.7 7.4 %analysis.1 = bf16[8,128,512]{2,1,0:T(8,128)(2,1)S(1)} custom-call(s32[2]{0:T(128)S(1)} %bitcast.12, bf16[8,2,32,512]{3,2,1,0:T(8,128)(2,1)S(1)} %all-to-all-done.refs_0_, f32[2,8,512]{2,1,0:T(8,128)S(1)} %constant_dynamic-slice_fusion.refs_1_, s32[2,512]{1,0:T(2,128)S(1)} %bitcast.11, bf16[8,128,512]{2,1,0:T(8,128)(2,1)S(1)} %all-to-all-done.1.refs_3_), custom_call_target="tpu_custom_call" | custom-call | tf_op jit(solution)/shard_map/analysis/pallas_call | solution.py:181
  73.1 19.5 %all_to_all.15 = bf16[8,128,512]{2,1,0:T(8,128)(2,1)S(1)} all-to-all(bf16[8,128,512]{2,1,0:T(8,128)(2,1)S(1)} %analysis.1), channel_id=1, replica_groups=mesh['member'=8,'space'=4] {'member'}, dimensions={0} | all-to-all | bytes 2097152 | tf_op jit(solution)/shard_map/all_to_all | solution.py:189
  92.6 0.6 copy.12
  93.2 1.6 %reshape.15 = bf16[32,4,4096]{2,1,0:T(4,128)(2,1)} reshape(bf16[128,8,512]{2,1,0:T(8,128)(2,1)S(1)} %copy.12) | data formatting | bytes 2097152 | tf_op jit(solution)/shard_map/reshape | solution.py:190
  (5 shorter events, 0.1 us)
Async XLA Ops:
  0.8 36.0 %collective-permute-start.2 = (f32[2,8192]{1,0:T(2,128)S(1)}, f32[2,8192]{1,0:T(2,128)S(1)}, u32[]{:S(2)}, u32[]{:S(2)}) collective-permute-start(f32[2,8192]{1,0:T(2,128)S(1)} %pad_maximum_fusion), channel_id=1, source_target_pairs={{0,1},{1,2},{2,3},{3,0},{4,5},{5,6},{6,7},{7,4},{8,9},{9,10},{10,1... | collective-permute-start | bytes 196616 | tf_op jit(solution)/shard_map/ppermute | solution.py:172
  3.0 33.8 %collective-permute-start.3 = (f32[2,8192]{1,0:T(2,128)S(1)}, f32[2,8192]{1,0:T(2,128)S(1)}, u32[]{:S(2)}, u32[]{:S(2)}) collective-permute-start(f32[2,8192]{1,0:T(2,128)S(1)} %pad_maximum_fusion), channel_id=1, source_target_pairs={{1,0},{2,1},{3,2},{0,3},{5,4},{6,5},{7,6},{4,7},{9,8},{10,9},{11,1... | collective-permute-start | bytes 196616 | tf_op jit(solution)/shard_map/ppermute | solution.py:172
  6.4 30.5 %collective-permute-start = (bf16[32,8192]{1,0:T(8,128)(2,1)S(1)}, bf16[32,8192]{1,0:T(8,128)(2,1)S(1)}, u32[]{:S(2)}, u32[]{:S(2)}) collective-permute-start(bf16[32,8192]{1,0:T(8,128)(2,1)S(1)} %convert_element_type.3.own_ref), channel_id=1, source_target_pairs={{0,1},{1,2},{2,3},{3,0},{4,5},{5,6},{6,7},{7,4},{8,9},{9,10},{10,1... | collective-permute-start | bytes 1572872 | tf_op jit(solution)/shard_map/ppermute | solution.py:169
  6.5 30.4 %collective-permute-start.1 = (bf16[32,8192]{1,0:T(8,128)(2,1)S(1)}, bf16[32,8192]{1,0:T(8,128)(2,1)S(1)}, u32[]{:S(2)}, u32[]{:S(2)}) collective-permute-start(bf16[32,8192]{1,0:T(8,128)(2,1)S(1)} %convert_element_type.3.own_ref), channel_id=1, source_target_pairs={{1,0},{2,1},{3,2},{0,3},{5,4},{6,5},{7,6},{4,7},{9,8},{10,9},{11,1... | collective-permute-start | bytes 1572872 | tf_op jit(solution)/shard_map/ppermute | solution.py:169
  12.8 5.6 %copy-start.2 = (f32[8192]{0:T(1024)S(1)}, f32[8192]{0:T(1024)}, u32[]{:S(2)}) copy-start(f32[8192]{0:T(1024)} %param.10) | copy-start | bytes 98308
  12.8 5.6 %copy-start.3 = (f32[8192]{0:T(1024)S(1)}, f32[8192]{0:T(1024)}, u32[]{:S(2)}) copy-start(f32[8192]{0:T(1024)} %param.9) | copy-start | bytes 98308
  12.8 41.9 %all-to-all-start.1 = ((bf16[8,128,512]{2,1,0:T(8,128)(2,1)}), bf16[8,128,512]{2,1,0:T(8,128)(2,1)S(1)}, u32[]{:S(2)}, u32[]{:S(2)}) async-start(bf16[8,128,512]{2,1,0:T(8,128)(2,1)} %bitcast.13), calls=%async_computation.1 | async-start | bytes 2097152 | tf_op jit(solution)/shard_map/all_to_all | solution.py:179
  18.4 0.7 copy-start.4
  54.7 10.3 %all-to-all-start = ((bf16[8,2,32,512]{3,2,1,0:T(8,128)(2,1)}), bf16[8,2,32,512]{3,2,1,0:T(8,128)(2,1)S(1)}, u32[]{:S(2)}, u32[]{:S(2)}) async-start(bf16[8,2,32,512]{3,2,1,0:T(8,128)(2,1)} %bitcast.4), calls=%async_computation | async-start | bytes 1048576 | tf_op jit(solution)/shard_map/all_to_all | solution.py:176
  58.3 6.8 %copy-start = (s32[1,2,512]{2,1,0:T(2,128)S(1)}, s32[1,2,512]{2,1,0:T(2,128)}, u32[]{:S(2)}) copy-start(s32[1,2,512]{2,1,0:T(2,128)} %param.13) | copy-start | bytes 12292
  65.1 0.7 copy-start.1

commit v2 on v1

--- a/solution.py
+++ b/solution.py
@@ -1,3 +1,5 @@
+import functools
+
 import jax
 import jax.numpy as jnp
 from jax import lax
@@ -20,9 +22,11 @@
         def _(c, k=k, src=src, side=side):
             for u in range(4):
                 at = pl.multiple_of(c * 512 + u * 128, 128)
+                line = c * 4 + u
                 x = jnp.concatenate(
-                    [src[:, pl.ds(at, 128)].astype(F32), side[:, pl.ds(at, 128)],
-                     jnp.zeros((128 - members - 8, 128), F32)], axis=0)
+                    [src[:, pl.ds(at, 128)].astype(F32), side[pl.ds(line, 1), :],
+                     side[pl.ds(line + tile_obs // 128, 1), :],
+                     jnp.zeros((128 - members - 2, 128), F32)], axis=0)
                 table[pl.ds(pl.multiple_of(k * tile_obs + at, 128), 128), :] = x.T
 
     @pl.loop(0, blocks)
@@ -142,19 +146,86 @@
     return (inc.reshape(n // 8, 8, cols) + mean[None]).reshape(n, cols).astype(BF16)
 
 
-def main_kernel(count_ref, levels, picks_ref, side_ref, bin_ref, field_ref, out_ref):
+def greet(devices, me, space, here):
+    barrier = pltpu.get_barrier_semaphore()
+    for k in range(1, devices):
+        pl.semaphore_signal(barrier, inc=1, device_id={"member": lax.rem(me + k, devices)},
+                            device_id_type=pl.DeviceIdType.MESH)
+    if space:
+        for k in (1, space - 1):
+            pl.semaphore_signal(barrier, inc=1, device_id={"space": lax.rem(here + k, space)},
+                                device_id_type=pl.DeviceIdType.MESH)
+    pl.semaphore_wait(barrier, devices - 1 + (2 if space else 0))
+
+
+def send(src, dst, sems, at, axis, target):
+    return pltpu.make_async_remote_copy(
+        src_ref=src, dst_ref=dst, send_sem=sems[0].at[at], recv_sem=sems[1].at[at],
+        device_id={axis: target}, device_id_type=pl.DeviceIdType.MESH)
+
+
+def exchange_kernel(devices, space, own_ref, side_ref, slot_ref, field_ref,
+                    before_ref, after_ref, sbefore_ref, safter_ref, slots_ref, fields_ref,
+                    halo_send, halo_recv, slot_send, slot_recv, field_send, field_recv, local):
+    me, here = lax.axis_index("member"), lax.axis_index("space")
+    cols = field_ref.shape[1] // devices
+    lines = slot_ref.shape[0]
+    window = lambda d: pl.ds(pl.multiple_of(d * cols, 128), cols)
+    mine = pl.ds(pl.multiple_of(me * lines, 8), lines)
+    keep = [pltpu.make_async_copy(slot_ref, slots_ref.at[mine], local.at[0]),
+            pltpu.make_async_copy(field_ref.at[:, window(me)], fields_ref.at[me], local.at[1])]
+    greet(devices, me, space, here)
+    halo = (halo_send, halo_recv)
+    up, down = lax.rem(here + 1, space), lax.rem(here + space - 1, space)
+    copies = [send(own_ref, before_ref, halo, 0, "space", up), send(own_ref, after_ref, halo, 1, "space", down),
+              send(side_ref, sbefore_ref, halo, 2, "space", up), send(side_ref, safter_ref, halo, 3, "space", down)]
+    for k in range(1, devices):
+        to = lax.rem(me + k, devices)
+        copies.append(send(slot_ref, slots_ref.at[mine], (slot_send, slot_recv), k, "member", to))
+    for k in range(1, devices):
+        to = lax.rem(me + k, devices)
+        copies.append(send(field_ref.at[:, window(to)], fields_ref.at[me], (field_send, field_recv), k, "member", to))
+    for copy in copies + keep:
+        copy.start()
+    for copy in copies + keep:
+        copy.wait()
+
+
+def main_kernel(levels, count_ref, picks_ref, side_ref, bin_ref, field_ref, out_ref,
+                met, made, pick_send, pick_recv, out_send, out_recv):
     parts, blocks, share, slots = picks_ref.shape
     members = parts * share
     rows, cols = field_ref.shape[0] * field_ref.shape[1], field_ref.shape[2]
     cut = cols // blocks
-    x = [picks_ref[:, b].reshape(members, slots).astype(F32) for b in range(blocks)]
+    me = lax.axis_index("member")
+    greet(parts, me, 0, 0)
+    copies = []
+    for k in range(1, parts):
+        to = lax.rem(me + k, parts)
+        copies.append(send(picks_ref.at[to], met.at[me], (pick_send, pick_recv), k, "member", to))
+    for copy in copies:
+        copy.start()
+    met[me] = picks_ref[me]
+    for copy in copies:
+        copy.wait()
+    x = [met[:, b].reshape(members, slots).astype(F32) for b in range(blocks)]
     zs, halves, pulls = roots(
         x, [side_ref[b, 0:1] for b in range(blocks)], [side_ref[b, 1:2] for b in range(blocks)],
         [bin_ref[b:b + 1] for b in range(blocks)], [count_ref[b] for b in range(blocks)])
+    copies = []
     for b in range(blocks):
         w4 = spread_levels(weights_t(zs[b], halves[b], pulls[b]), levels)
         f = field_ref[:, :, b * cut:(b + 1) * cut].reshape(rows, cut)
-        out_ref[:, :, b * cut:(b + 1) * cut] = analyse(f, w4, levels).reshape(parts, rows // parts, cut)
+        made[b] = analyse(f, w4, levels).reshape(parts, rows // parts, cut)
+        window = pl.ds(pl.multiple_of(me * cols + b * cut, 128), cut)
+        for k in range(1, parts):
+            to = lax.rem(me + k, parts)
+            copy = send(made.at[b, to], out_ref.at[:, window], (out_send.at[b], out_recv.at[b]), k, "member", to)
+            copy.start()
+            copies.append(copy)
+        out_ref[:, window] = made[b, me]
+    for copy in copies:
+        copy.wait()
 
 
 def per_device(background, obs_ens, observed, variance, obs_slot, obs_count, loc_bin):
@@ -162,32 +233,40 @@
     space = lax.axis_size("space")
     share, levels, columns = background.shape
     blocks, width = obs_slot.shape[1:]
-    up = [(i, (i + 1) % space) for i in range(space)]
-    down = [(j, i) for i, j in up]
+    rows, cols = share * levels, columns // devices
     own = obs_ens.astype(BF16)
-    side = jnp.concatenate([observed[None], variance[None], jnp.zeros((6, observed.shape[0]), F32)], axis=0)
-    tables = (lax.ppermute(own, "space", up), own, lax.ppermute(own, "space", down))
-    short = side[:2]
-    grow = lambda s: jnp.concatenate([s, jnp.zeros((6, s.shape[1]), F32)], axis=0)
-    sides = (grow(lax.ppermute(short, "space", up)), side, grow(lax.ppermute(short, "space", down)))
-    every_slot = lax.all_gather(obs_slot[0], "member", axis=0, tiled=True).reshape(-1)
-    picked, picked_side = pick(every_slot, tables, sides, devices * blocks, width)
+    side = jnp.concatenate([observed.reshape(-1, 128), variance.reshape(-1, 128)], axis=0)
+    slots = obs_slot.reshape(-1, 128)
+    flat = background.reshape(rows, columns)
+    hbm = pl.BlockSpec(memory_space=pl.ANY)
+    vmem = pl.BlockSpec(memory_space=pltpu.VMEM)
+    dma = lambda *n: pltpu.SemaphoreType.DMA(n)
+    like = jax.ShapeDtypeStruct
+    before, after, sbefore, safter, every_slot, fields = pl.pallas_call(
+        functools.partial(exchange_kernel, devices, space),
+        out_shape=(like(own.shape, BF16), like(own.shape, BF16), like(side.shape, F32), like(side.shape, F32),
+                   like((devices * slots.shape[0], 128), jnp.int32), like((devices, rows, cols), BF16)),
+        in_specs=[hbm] * 4,
+        out_specs=(hbm,) * 6,
+        scratch_shapes=[dma(4), dma(4), dma(devices), dma(devices), dma(devices), dma(devices), dma(2)],
+        compiler_params=pltpu.CompilerParams(collective_id=0, has_side_effects=True),
+        name="exchange",
+    )(own, side, slots, flat)
+    picked, picked_side = pick(every_slot.reshape(-1), (before, own, after), (sbefore, side, safter),
+                               devices * blocks, width)
     picked = picked.reshape(devices, blocks, share, width)
-    picks = lax.all_to_all(picked, "member", split_axis=0, concat_axis=0, tiled=True)
     mine = lax.dynamic_slice_in_dim(picked_side, lax.axis_index("member") * blocks, blocks, 0)
-    flat = background.reshape(share * levels, devices, columns // devices).transpose(1, 0, 2)
-    fields = lax.all_to_all(flat, "member", split_axis=0, concat_axis=0, tiled=True)
-    vmem = pl.BlockSpec(memory_space=pltpu.VMEM)
     out = pl.pallas_call(
-        lambda c, *refs: main_kernel(c, levels, *refs),
-        out_shape=jax.ShapeDtypeStruct(fields.shape, BF16),
+        functools.partial(main_kernel, levels),
+        out_shape=like((rows, columns), BF16),
         in_specs=[pl.BlockSpec(memory_space=pltpu.SMEM)] + [vmem] * 4,
         out_specs=vmem,
-        compiler_params=pltpu.CompilerParams(vmem_limit_bytes=50 * 2**20),
+        scratch_shapes=[pltpu.VMEM(picked.shape, BF16), pltpu.VMEM((blocks, devices, rows, cols // blocks), BF16),
+                        dma(devices), dma(devices), dma(blocks, devices), dma(blocks, devices)],
+        compiler_params=pltpu.CompilerParams(collective_id=1, has_side_effects=True, vmem_limit_bytes=50 * 2**20),
         name="analysis",
-    )(obs_count[0], picks, mine, loc_bin[0], fields)
-    back = lax.all_to_all(out, "member", split_axis=0, concat_axis=0, tiled=True)
-    return back.transpose(1, 0, 2).reshape(share, levels, columns)
+    )(obs_count[0], picked, mine, loc_bin[0], fields)
+    return out.reshape(share, levels, columns)
 
 
 def solution(mesh):

time: 96.6 us -> 91 us (0.942); the launches traced: 94.8 us -> 90.6 us
  Pallas kernels: 25.2 us -> 79.5 us
  blocking collectives: 37.2 us -> 0 us
  starting transfers between devices: 16.7 us -> 0 us
  waiting for transfers between devices: 6.76 us -> 0 us
  local copies, waits for them, and re-layouts: 6.64 us -> 8.19 us
    pallas_call x1 -> x2, Pallas kernels: 7.39 us -> 62.5 us  [the longest x1 32.3 us: per_device(): pl.pallas_call(functools.partial(exchange_kernel, devices, space), out_sh...]
    all_to_all x1 -> x0, blocking collectives: 19.5 us -> none  [per_device(): lax.all_to_all(out, 'member', split_axis=0, concat_axis=0, tiled=True)]
    all_gather x1 -> x0, blocking collectives: 17.7 us -> none  [per_device(): lax.all_gather(obs_slot[0], 'member', axis=0, tiled=True).reshape(-1)]
    all_to_all x2 -> x0, starting transfers between devices: 9.1 us -> none  [the longest x1 5.52 us: per_device(): lax.all_to_all(flat, 'member', split_axis=0, concat_axis=0, tiled=True)]
    ppermute x4 -> x0, starting transfers between devices: 7.58 us -> none  [the longest x1 3.25 us: per_device(): lax.ppermute(own, 'space', down)]
    all_to_all x2 -> x0, waiting for transfers between devices: 6.75 us -> none  [the longest x1 6.75 us: per_device(): lax.all_to_all(picked, 'member', split_axis=0, concat_axis=0, tiled=True)]
    unnamed x11 -> x28, local copies, waits for them, and re-layouts: 1.26 us -> 5.29 us
    reshape x3, local copies, waits for them, and re-layouts: 4.67 us -> 2.89 us  [the longest x1 1.21 us: per_device(): return out.reshape(share, levels, columns)]
  transfers between devices with their start and end apart: 6 -> 0, of which waited for: 1 -> 0; matrix products, arithmetic and copies ran while one was open for 5% -> 0% of each run, Pallas kernels for 19% -> 0%
where the time goes in v2:
time: 91 us; the launch traced here: 90.6 us
  Pallas kernels  79.5 us (87%)
  local copies, waits for them, and re-layouts  8.19 us (9%)
  other arithmetic  2.81 us (3%)
    pallas_call x1, Pallas kernels, per_device(): pl.pallas_call(functools.partial(exchange_kernel, devices, space), out_sh...  32.3 us
    pallas_call x1, Pallas kernels, per_device(): pl.pallas_call(functools.partial(main_kernel, levels), out_shape=like((ro...  30.1 us
    pallas_call x1, Pallas kernels, pick(): pl.pallas_call(pick_kernel, out_shape=(jax.ShapeDtypeStruct((blocks, memb...  17 us
    unnamed x28, local copies, waits for them, and re-layouts  5.29 us
    convert_element_type x1, other arithmetic, per_device(): own = obs_ens.astype(BF16)  2.2 us

profile of v2, /device:TPU:1, one launch (start us, length us, event | category | flops | bytes accessed | tf_op | source)
XLA Modules:
  0.0 90.6 jit_solution(9886084112950187458)
XLA Ops:
  0.0 0.0 copy-start.12
  0.0 0.0 copy-start.11
  0.0 0.0 copy-start.10
  0.0 2.2 %convert_element_type.3.own_ref = bf16[32,8192]{1,0:T(8,128)(2,1)} convert(f32[32,8192]{1,0:T(8,128)} %param.8) | non-fusion elementwise | flops 262144 | bytes 1572864 | tf_op jit(solution)/shard_map/convert_element_type | solution.py:237
  2.2 0.0 copy-done.12
  2.2 0.0 copy-done.11
  2.2 0.6 pad_maximum_fusion.side_ref.sown_ref
  2.8 0.0 copy-done.10
  2.8 0.0 copy-start.13
  2.8 1.1 %reshape.24.field_ref = bf16[128,4096]{1,0:T(8,128)(2,1)} reshape(bf16[32,4,4096]{2,1,0:T(4,128)(2,1)S(1)} %copy-done.10) | data formatting | bytes 2097152 | tf_op jit(solution)/shard_map/reshape | solution.py:240
  3.9 0.0 copy-done.13
  3.9 0.6 reshape.23.slot_ref
  4.5 0.0 copy-start
  4.5 0.0 copy-start.2
  4.5 32.3 %exchange.1 = (bf16[32,8192]{1,0:T(8,128)(2,1)}, bf16[32,8192]{1,0:T(8,128)(2,1)}, f32[128,128]{1,0:T(8,128)}, f32[128,128]{1,0:T(8,128)}, s32[64,128]{1,0:T(8,128)}, /*index=5*/bf16[8,128,512]{2,1,0:T(8,128)(2,1)}) custom-call(bf16[32,8192]{1,0:T(8,128)(2,1)} %convert_element_type.3.own_ref, f32[128,128]{1,0:T(8,128)} %pad_maximum_fusion.side_ref.sown_ref, ...), custom_call_target="tpu_custom_call" | custom-call | tf_op jit(solution)/shard_map/exchange/pallas_call | solution.py:245
  36.9 0.0 copy-start.1
  36.9 0.0 copy-done
  36.9 0.0 copy-done.2
  36.9 0.0 copy-start.3
  36.9 1.1 %copy-done.3 = bf16[32,8192]{1,0:T(8,128)(2,1)S(1)} copy-done((bf16[32,8192]{1,0:T(8,128)(2,1)S(1)}, bf16[32,8192]{1,0:T(8,128)(2,1)}, u32[]{:S(2)}) %copy-start.3) | copy-done | bytes 524312
  38.0 0.0 copy-start.4
  38.0 1.0 %copy-done.4 = bf16[32,8192]{1,0:T(8,128)(2,1)S(1)} copy-done((bf16[32,8192]{1,0:T(8,128)(2,1)S(1)}, bf16[32,8192]{1,0:T(8,128)(2,1)}, u32[]{:S(2)}) %copy-start.4) | copy-done | bytes 524312
  39.1 0.0 copy-start.5
  39.1 0.8 copy-done.5
  39.9 0.0 copy-start.6
  39.9 0.8 copy-done.6
  40.8 0.0 copy-start.7
  40.8 0.8 copy-done.7
  41.5 17.0 %pick.1 = (bf16[16,32,512]{2,1,0:T(8,128)(2,1)S(1)}, f32[16,8,512]{2,1,0:T(8,128)S(1)}) custom-call(s32[8192]{0:T(1024)S(1)} %bitcast.7, bf16[32,8192]{1,0:T(8,128)(2,1)S(1)} %copy-done.3, bf16[32,8192]{1,0:T(8,128)(2,1)S(1)} %copy-done, bf16[32,8192]{1,0:T(8,128)(2,1)S(1)} %copy-done.4, f32[128,128]{1,0:T(8,128)S(1)} %copy-done.5, ...), custom_call_target="tpu_custom_call" | custom-call | tf_op jit(solution)/shard_map/pick/pallas_call | solution.py:49
  58.6 0.0 copy-start.8
  58.6 0.0 copy-start.9
  58.6 0.0 copy-done.1
  58.6 0.7 copy-done.8
  59.3 0.0 copy-done.9
  59.3 30.1 %analysis.1 = bf16[128,4096]{1,0:T(8,128)(2,1)S(1)} custom-call(s32[2]{0:T(128)S(1)} %bitcast.9, bf16[8,2,32,512]{3,2,1,0:T(8,128)(2,1)S(1)} %bitcast.6, f32[2,8,512]{2,1,0:T(8,128)S(1)} %constant_dynamic-slice_fusion.side_ref, s32[2,512]{1,0:T(2,128)S(1)} %bitcast.8, bf16[8,128,512]{2,1,0:T(8,128)(2,1)S(1)} %copy-done.1), custom_call_target="tpu_custom_call" | custom-call | tf_op jit(solution)/shard_map/analysis/pallas_call | solution.py:259
  89.4 1.2 %reshape.27 = bf16[32,4,4096]{2,1,0:T(4,128)(2,1)} reshape(bf16[128,4096]{1,0:T(8,128)(2,1)S(1)} %analysis.1) | data formatting | bytes 2097152 | tf_op jit(solution)/shard_map/reshape | solution.py:269
  (1 shorter events, 0.0 us)
Async XLA Ops:
  0.0 2.2 %copy-start.12 = (f32[8192]{0:T(1024)S(1)}, f32[8192]{0:T(1024)}, u32[]{:S(2)}) copy-start(f32[8192]{0:T(1024)} %param.9) | copy-start | bytes 98308
  0.0 2.2 %copy-start.11 = (f32[8192]{0:T(1024)S(1)}, f32[8192]{0:T(1024)}, u32[]{:S(2)}) copy-start(f32[8192]{0:T(1024)} %param.10) | copy-start | bytes 98308
  0.0 2.8 %copy-start.10 = (bf16[32,4,4096]{2,1,0:T(4,128)(2,1)S(1)}, bf16[32,4,4096]{2,1,0:T(4,128)(2,1)}, u32[]{:S(2)}) copy-start(bf16[32,4,4096]{2,1,0:T(4,128)(2,1)} %param.7) | copy-start | bytes 3145732
  2.8 1.1 %copy-start.13 = (s32[1,2,512]{2,1,0:T(2,128)S(1)}, s32[1,2,512]{2,1,0:T(2,128)}, u32[]{:S(2)}) copy-start(s32[1,2,512]{2,1,0:T(2,128)} %param.11) | copy-start | bytes 12292
  4.5 32.4 %copy-start = (bf16[32,8192]{1,0:T(8,128)(2,1)S(1)}, bf16[32,8192]{1,0:T(8,128)(2,1)}, u32[]{:S(2)}) copy-start(bf16[32,8192]{1,0:T(8,128)(2,1)} %convert_element_type.3.own_ref) | copy-start | bytes 1572868
  4.5 32.4 %copy-start.2 = (f32[128,128]{1,0:T(8,128)S(1)}, f32[128,128]{1,0:T(8,128)}, u32[]{:S(2)}) copy-start(f32[128,128]{1,0:T(8,128)} %pad_maximum_fusion.side_ref.sown_ref) | copy-start | bytes 196612
  36.9 21.7 %copy-start.1 = (bf16[8,128,512]{2,1,0:T(8,128)(2,1)S(1)}, bf16[8,128,512]{2,1,0:T(8,128)(2,1)}, u32[]{:S(2)}) copy-start(bf16[8,128,512]{2,1,0:T(8,128)(2,1)} %get-tuple-element.20.field_ref) | copy-start | bytes 3145732
  36.9 1.1 %copy-start.3 = (bf16[32,8192]{1,0:T(8,128)(2,1)S(1)}, bf16[32,8192]{1,0:T(8,128)(2,1)}, u32[]{:S(2)}) copy-start(bf16[32,8192]{1,0:T(8,128)(2,1)} %get-tuple-element.14.before_ref) | copy-start | bytes 1572868
  38.0 1.0 %copy-start.4 = (bf16[32,8192]{1,0:T(8,128)(2,1)S(1)}, bf16[32,8192]{1,0:T(8,128)(2,1)}, u32[]{:S(2)}) copy-start(bf16[32,8192]{1,0:T(8,128)(2,1)} %get-tuple-element.15.after_ref) | copy-start | bytes 1572868
  39.1 0.8 copy-start.5
  39.9 0.8 copy-start.6
  40.8 0.8 copy-start.7
  58.6 0.7 copy-start.8
  58.6 0.7 copy-start.9

commit v3 on v2

v3 whole, which is shorter than its diff:
```python
import functools

import jax
import jax.numpy as jnp
from jax import lax
from jax.experimental import pallas as pl
from jax.experimental.pallas import tpu as pltpu
from jax.sharding import PartitionSpec as P

ITERS = 8
NBINS = 32
F32 = jnp.float32
BF16 = jnp.bfloat16


def fill(table, src, side, base):
    members, tile_obs = src.shape

    @pl.loop(0, tile_obs // 512)
    def _(c):
        for u in range(4):
            at = pl.multiple_of(c * 512 + u * 128, 128)
            line = c * 4 + u
            x = jnp.concatenate(
                [src[:, pl.ds(at, 128)].astype(F32), side[pl.ds(line, 1), :],
                 side[pl.ds(line + tile_obs // 128, 1), :],
                 jnp.zeros((128 - members - 2, 128), F32)], axis=0)
            table[pl.ds(pl.multiple_of(base + at, 128), 128), :] = x.T


def dot1(a, b, nt=False):
    dims = (((1,), (1 if nt else 0,)), ((), ()))
    return lax.dot_general(a.astype(BF16), b.astype(BF16), dims, preferred_element_type=F32)


def dot3(a, b):
    ah, bh = a.astype(BF16), b.astype(BF16)
    al, bl = (a - ah.astype(F32)).astype(BF16), (b - bh.astype(F32)).astype(BF16)
    return dot1(ah, bh) + (dot1(ah, bl) + dot1(al, bh))


def eye(n):
    return (lax.broadcasted_iota(jnp.int32, (n, n), 0) == lax.broadcasted_iota(jnp.int32, (n, n), 1)).astype(F32)


def roots(x, observed, variance, loc_bin, count):
    members, slots = x[0].shape
    ident = eye(members)
    ys, zs, halves, pulls = [], [], [], []
    for b in range(len(x)):
        mean = jnp.sum(x[b], axis=0, keepdims=True) * (1.0 / members)
        pert = x[b] - mean
        scaled = loc_bin[b].astype(F32) / (NBINS * 0.375)
        weight = jnp.exp(-0.5 * scaled * scaled) / variance[b]
        weight = jnp.where(lax.broadcasted_iota(jnp.int32, (1, slots), 1) < count[b], weight, 0.0)
        root_w = pert * jnp.sqrt(weight)
        gram = dot1(root_w, root_w, nt=True)
        system = gram + (members - 1.0) * ident
        half = 0.5 * jnp.sum(system * ident)
        pulls.append(jnp.sum(pert * (weight * (observed[b] - mean)), axis=1, keepdims=True))
        halves.append(half)
        ys.append(system / half)
        zs.append(None)
    for sweep in range(ITERS):
        for b in range(len(x)):
            y, z = ys[b], zs[b]
            if z is None:
                m = y
                zs[b] = 1.5 * ident - 0.5 * m
                ys[b] = 1.5 * y - 0.5 * dot1(y, m)
                continue
            m = dot1(z, y) if sweep < ITERS - 2 else dot3(z, y)
            if sweep < ITERS - 3:
                zs[b] = 1.5 * z - 0.5 * dot1(m, z)
                ys[b] = 1.5 * y - 0.5 * dot1(y, m)
            else:
                e = ident - m
                zs[b] = z + 0.5 * dot1(e, z)
                if sweep < ITERS - 1:
                    ys[b] = y + 0.5 * dot1(y, e)
    return zs, halves, pulls


def weights_t(z, half, pulled):
    members = z.shape[0]
    ident = eye(members)
    inner = jnp.sum(z * pulled, axis=0, keepdims=True)
    shift = jnp.sum(z * inner, axis=1, keepdims=True) / half
    shift_row = jnp.sum(shift * ident, axis=0, keepdims=True)
    return (jnp.sqrt((members - 1.0) / half) * z + shift_row).astype(BF16)


def spread_levels(wt, levels):
    members = wt.shape[0]
    n = members * levels
    r0 = lax.broadcasted_iota(jnp.int32, (n, members), 0) // levels
    up = (r0 == lax.broadcasted_iota(jnp.int32, (n, members), 1)).astype(BF16)
    tall = dot1(up, wt)
    wide = dot1(tall, up, nt=True)
    same = (lax.broadcasted_iota(jnp.int32, (n, n), 0) % levels) == (lax.broadcasted_iota(jnp.int32, (n, n), 1) % levels)
    return jnp.where(same, wide, 0.0).astype(BF16)


def analyse(f, w4, levels):
    n, cols = f.shape
    members = n // levels
    f = f.astype(F32).reshape(n // 8, 8, cols)
    total = jnp.sum(f, axis=0)
    step = levels
    while step < 8:
        total = total + pltpu.roll(total, step, 0)
        step *= 2
    mean = total * (1.0 / members)
    pert = (f - mean[None]).reshape(n, cols)
    inc = dot1(w4, pert)
    return (inc.reshape(n // 8, 8, cols) + mean[None]).reshape(n, cols).astype(BF16)


def greet(devices, me, space, here):
    barrier = pltpu.get_barrier_semaphore()
    for k in range(1, devices):
        pl.semaphore_signal(barrier, inc=1, device_id={"member": lax.rem(me + k, devices)},
                            device_id_type=pl.DeviceIdType.MESH)
    if space:
        for k in (1, space - 1):
            pl.semaphore_signal(barrier, inc=1, device_id={"space": lax.rem(here + k, space)},
                                device_id_type=pl.DeviceIdType.MESH)
    pl.semaphore_wait(barrier, devices - 1 + (2 if space else 0))


def send(src, dst, sems, at, axis, target):
    return pltpu.make_async_remote_copy(
        src_ref=src, dst_ref=dst, send_sem=sems[0].at[at], recv_sem=sems[1].at[at],
        device_id={axis: target}, device_id_type=pl.DeviceIdType.MESH)


def main_kernel(devices, space, levels, count_ref, own_ref, side_ref, slot_ref, bin_ref, field_ref, out_ref,
                table, picked_rows, before, after, sbefore, safter, slots_met, slots_smem, fields,
                picks, met, side_met, made, local, halo_send, halo_recv, slot_send, slot_recv,
                field_send, field_recv, pick_send, pick_recv, out_send, out_recv):
    parts, blocks, share, slots = picks.shape
    members = parts * share
    tile_obs = own_ref.shape[1]
    rows, cols = fields.shape[0] * fields.shape[1], fields.shape[2]
    cut = cols // blocks
    me, here = lax.axis_index("member"), lax.axis_index("space")
    lines = slot_ref.shape[0]
    per = lines // blocks
    window = lambda d: pl.ds(pl.multiple_of(d * cols, 128), cols)
    mine = pl.ds(pl.multiple_of(me * lines, 8), lines)
    keep = pltpu.make_async_copy(field_ref.at[:, window(me)], fields.at[me], local.at[0])
    keep.start()
    greet(devices, me, space, here)
    halo = (halo_send, halo_recv)
    up, down = lax.rem(here + 1, space), lax.rem(here + space - 1, space)
    halo_copies = [send(own_ref, before, halo, 0, "space", up), send(own_ref, after, halo, 1, "space", down),
                   send(side_ref, sbefore, halo, 2, "space", up), send(side_ref, safter, halo, 3, "space", down)]
    for copy in halo_copies:
        copy.start()
    slot_copies, field_copies, pick_copies = [], [], []
    for k in range(1, devices):
        to = lax.rem(me + k, devices)
        slot_copies.append(send(slot_ref, slots_met.at[mine], (slot_send, slot_recv), k, "member", to))
        field_copies.append(send(field_ref.at[:, window(to)], fields.at[me], (field_send, field_recv), k, "member", to))
        pick_copies.append(send(picks.at[to], met.at[me], (pick_send, pick_recv), k, "member", to))
    for copy in slot_copies:
        copy.start()
    slots_met[mine, :] = slot_ref[...]
    fill(table, own_ref, side_ref, tile_obs)
    for copy in slot_copies:
        copy.wait()
    to_smem = pltpu.make_async_copy(slots_met, slots_smem, local.at[1])
    to_smem.start()
    to_smem.wait()
    for copy in halo_copies:
        copy.wait()
    for copy in field_copies:
        copy.start()
    fill(table, before, sbefore, 0)
    fill(table, after, safter, 2 * tile_obs)

    def pick_for(to, own):
        @pl.loop(0, lines)
        def _(r):
            for u in range(128):
                i = slots_smem[to * lines + r, u]
                picked_rows[u:u + 1, :] = table[pl.ds(i, 1), :]
            t = picked_rows[...].T
            block = r // per
            at = pl.ds(pl.multiple_of((r % per) * 128, 128), 128)
            if own:
                met[to, block, :, at] = t[:share].astype(BF16)
                side_met[block, :, at] = t[share:share + 8]
            else:
                picks[to, block, :, at] = t[:share].astype(BF16)

    @pl.loop(1, devices)
    def _(k):
        to = lax.rem(me + k, devices)
        pick_for(to, False)
        send(picks.at[to], met.at[me], (pick_send, pick_recv), k, "member", to).start()

    pick_for(me, True)
    for copy in pick_copies:
        copy.wait()
    x = [met[:, b].reshape(members, slots).astype(F32) for b in range(blocks)]
    zs, halves, pulls = roots(
        x, [side_met[b, 0:1] for b in range(blocks)], [side_met[b, 1:2] for b in range(blocks)],
        [bin_ref[b:b + 1] for b in range(blocks)], [count_ref[b] for b in range(blocks)])
    keep.wait()
    for copy in field_copies:
        copy.wait()
    copies = []
    for b in range(blocks):
        w4 = spread_levels(weights_t(zs[b], halves[b], pulls[b]), levels)
        f = fields[:, :, b * cut:(b + 1) * cut].reshape(rows, cut)
        made[b] = analyse(f, w4, levels).reshape(parts, rows // parts, cut)
        window = pl.ds(pl.multiple_of(me * cols + b * cut, 128), cut)
        for k in range(1, parts):
            to = lax.rem(me + k, parts)
            copy = send(made.at[b, to], out_ref.at[:, window], (out_send.at[b], out_recv.at[b]), k, "member", to)
            copy.start()
            copies.append(copy)
        out_ref[:, window] = made[b, me]
    for copy in copies:
        copy.wait()


def per_device(background, obs_ens, observed, variance, obs_slot, obs_count, loc_bin):
    devices = lax.axis_size("member")
    space = lax.axis_size("space")
    share, levels, columns = background.shape
    blocks, width = obs_slot.shape[1:]
    rows, cols = share * levels, columns // devices
    own = obs_ens.astype(BF16)
    side = jnp.concatenate([observed.reshape(-1, 128), variance.reshape(-1, 128)], axis=0)
    slots = obs_slot.reshape(-1, 128)
    flat = background.reshape(rows, columns)
    hbm = pl.BlockSpec(memory_space=pl.ANY)
    vmem = pl.BlockSpec(memory_space=pltpu.VMEM)
    dma = lambda *n: pltpu.SemaphoreType.DMA(n)
    like = jax.ShapeDtypeStruct
    out = pl.pallas_call(
        functools.partial(main_kernel, devices, space, levels),
        out_shape=like((rows, columns), BF16),
        in_specs=[pl.BlockSpec(memory_space=pltpu.SMEM)] + [vmem] * 4 + [hbm],
        out_specs=vmem,
        scratch_shapes=[
            pltpu.VMEM((3 * own.shape[1], 128), F32), pltpu.VMEM((128, 128), F32),
            pltpu.VMEM(own.shape, BF16), pltpu.VMEM(own.shape, BF16),
            pltpu.VMEM(side.shape, F32), pltpu.VMEM(side.shape, F32),
            pltpu.VMEM((devices * slots.shape[0], 128), jnp.int32), pltpu.SMEM((devices * slots.shape[0], 128), jnp.int32),
            pltpu.VMEM((devices, rows, cols), BF16),
            pltpu.VMEM((devices, blocks, share, width), BF16), pltpu.VMEM((devices, blocks, share, width), BF16),
            pltpu.VMEM((blocks, 8, width), F32), pltpu.VMEM((blocks, devices, rows, cols // blocks), BF16),
            dma(2), dma(4), dma(4)] + [dma(devices)] * 6 + [dma(blocks, devices)] * 2,
        compiler_params=pltpu.CompilerParams(collective_id=0, has_side_effects=True, vmem_limit_bytes=50 * 2**20),
        name="analysis",
    )(obs_count[0], own, side, slots, loc_bin[0], flat)
    return out.reshape(share, levels, columns)


def solution(mesh):
    in_specs = (
        P("member", None, "space"), P("member", "space"), P("space"), P("space"),
        P("space", "member", None), P("space", "member"), P("space", "member", None),
    )
    return jax.shard_map(per_device, mesh=mesh, in_specs=in_specs,
                         out_specs=P("member", None, "space"), check_vma=False)
```

time: 91 us -> 76.3 us (0.84)
  Pallas kernels: 79.5 us -> 71.4 us
  local copies, waits for them, and re-layouts: 8.19 us -> 2.58 us
    pallas_call x3 -> x1, Pallas kernels: 79.5 us -> 71.4 us  [per_device(): pl.pallas_call(functools.partial(main_kernel, devices, space, levels), ou...]
    unnamed x28 -> x8, local copies, waits for them, and re-layouts: 5.29 us -> 1.08 us
    convert_element_type x1, other arithmetic: 2.2 us -> 1.28 us  [per_device(): own = obs_ens.astype(BF16)]
where the time goes in v3:
time: 76.3 us; the launch traced here: 76 us
  Pallas kernels  71.4 us (94%)
  local copies, waits for them, and re-layouts  2.58 us (3%)
  other arithmetic  2.06 us (3%)
    pallas_call x1, Pallas kernels, per_device(): pl.pallas_call(functools.partial(main_kernel, devices, space, levels), ou...  71.4 us

profile of v3, /device:TPU:1, one launch (start us, length us, event | category | flops | bytes accessed | tf_op | source)
XLA Modules:
  0.0 76.0 jit_solution(17326098953684044421)
XLA Ops:
  0.0 0.0 copy-start.3
  0.0 0.0 copy-start.2
  0.0 0.7 copy-done.3
  0.7 0.8 %pad_maximum_fusion.side_ref = f32[128,128]{1,0:T(8,128)S(1)} fusion(f32[64,128]{1,0:T(8,128)} %bitcast.6, f32[64,128]{1,0:T(8,128)} %bitcast.7), kind=kLoop, calls=%fused_computation | loop fusion | flops 16384 | bytes 131072 | tf_op jit(solution)/shard_map/concatenate | solution.py:236
  1.5 1.3 %convert_element_type.3.own_ref = bf16[32,8192]{1,0:T(8,128)(2,1)S(1)} convert(f32[32,8192]{1,0:T(8,128)} %param.8) | non-fusion elementwise | flops 262144 | bytes 1572864 | tf_op jit(solution)/shard_map/convert_element_type | solution.py:235
  2.8 0.0 copy-done.2
  2.8 0.0 copy-start
  2.8 0.0 copy-start.1
  2.8 0.3 reshape.18.field_ref
  3.1 0.4 copy-done
  3.5 0.0 copy-done.1
  3.5 71.4 %analysis.1 = bf16[128,4096]{1,0:T(8,128)(2,1)S(1)} custom-call(s32[2]{0:T(128)S(1)} %bitcast.5, bf16[32,8192]{1,0:T(8,128)(2,1)S(1)} %convert_element_type.3.own_ref, f32[128,128]{1,0:T(8,128)S(1)} %pad_maximum_fusion.side_ref, s32[8,128]{1,0:T(8,128)S(1)} %reshape.17.slot_ref, s32[2,512]{1,0:T(2,128)S(1)} %bitcast.4, bf16[128,4096]{1,0:T(8,128)(2,1)S(1)} %reshape.18.field_ref), custom_call_target="tpu_custom_call" | custom-call | tf_op jit(solution)/shard_map/analysis/pallas_call | solution.py:243
  74.8 1.2 %reshape.19 = bf16[32,4,4096]{2,1,0:T(4,128)(2,1)} reshape(bf16[128,4096]{1,0:T(8,128)(2,1)S(1)} %analysis.1) | data formatting | bytes 2097152 | tf_op jit(solution)/shard_map/reshape | solution.py:260
  (1 shorter events, 0.0 us)
Async XLA Ops:
  0.0 0.7 copy-start.3
  0.0 2.8 %copy-start.2 = (bf16[32,4,4096]{2,1,0:T(4,128)(2,1)S(1)}, bf16[32,4,4096]{2,1,0:T(4,128)(2,1)}, u32[]{:S(2)}) copy-start(bf16[32,4,4096]{2,1,0:T(4,128)(2,1)} %param.7) | copy-start | bytes 3145732
  2.8 0.7 copy-start
  2.8 0.7 copy-start.1

commit v4 on v3

--- a/solution.py
+++ b/solution.py
@@ -9,14 +9,15 @@
 
 ITERS = 8
 NBINS = 32
+CHUNKS = 4
 F32 = jnp.float32
 BF16 = jnp.bfloat16
 
 
-def fill(table, src, side, base):
+def fill(table, src, side, base, first, width):
     members, tile_obs = src.shape
 
-    @pl.loop(0, tile_obs // 512)
+    @pl.loop(first // 512, (first + width) // 512)
     def _(c):
         for u in range(4):
             at = pl.multiple_of(c * 512 + u * 128, 128)
@@ -153,9 +154,14 @@
     greet(devices, me, space, here)
     halo = (halo_send, halo_recv)
     up, down = lax.rem(here + 1, space), lax.rem(here + space - 1, space)
-    halo_copies = [send(own_ref, before, halo, 0, "space", up), send(own_ref, after, halo, 1, "space", down),
-                   send(side_ref, sbefore, halo, 2, "space", up), send(side_ref, safter, halo, 3, "space", down)]
-    for copy in halo_copies:
+    side_copies = [send(side_ref, sbefore, halo, 0, "space", up), send(side_ref, safter, halo, 1, "space", down)]
+    piece = tile_obs // CHUNKS
+    halo_copies = []
+    for c in range(CHUNKS):
+        part = pl.ds(c * piece, piece)
+        halo_copies.append(send(own_ref.at[:, part], before.at[:, part], halo, 2 + 2 * c, "space", up))
+        halo_copies.append(send(own_ref.at[:, part], after.at[:, part], halo, 3 + 2 * c, "space", down))
+    for copy in side_copies + halo_copies:
         copy.start()
     slot_copies, field_copies, pick_copies = [], [], []
     for k in range(1, devices):
@@ -166,18 +172,22 @@
     for copy in slot_copies:
         copy.start()
     slots_met[mine, :] = slot_ref[...]
-    fill(table, own_ref, side_ref, tile_obs)
+    fill(table, own_ref, side_ref, tile_obs, 0, tile_obs)
     for copy in slot_copies:
         copy.wait()
     to_smem = pltpu.make_async_copy(slots_met, slots_smem, local.at[1])
     to_smem.start()
     to_smem.wait()
-    for copy in halo_copies:
-        copy.wait()
-    for copy in field_copies:
-        copy.start()
-    fill(table, before, sbefore, 0)
-    fill(table, after, safter, 2 * tile_obs)
+    for copy in side_copies:
+        copy.wait()
+    for c in range(CHUNKS):
+        halo_copies[2 * c].wait()
+        fill(table, before, sbefore, 0, c * piece, piece)
+        halo_copies[2 * c + 1].wait()
+        if c == CHUNKS - 1:
+            for copy in field_copies:
+                copy.start()
+        fill(table, after, safter, 2 * tile_obs, c * piece, piece)
 
     def pick_for(to, own):
         @pl.loop(0, lines)
@@ -203,16 +213,16 @@
     pick_for(me, True)
     for copy in pick_copies:
         copy.wait()
-    x = [met[:, b].reshape(members, slots).astype(F32) for b in range(blocks)]
-    zs, halves, pulls = roots(
-        x, [side_met[b, 0:1] for b in range(blocks)], [side_met[b, 1:2] for b in range(blocks)],
-        [bin_ref[b:b + 1] for b in range(blocks)], [count_ref[b] for b in range(blocks)])
-    keep.wait()
-    for copy in field_copies:
-        copy.wait()
     copies = []
     for b in range(blocks):
-        w4 = spread_levels(weights_t(zs[b], halves[b], pulls[b]), levels)
+        x = met[:, b].reshape(members, slots).astype(F32)
+        zs, halves, pulls = roots(
+            [x], [side_met[b, 0:1]], [side_met[b, 1:2]], [bin_ref[b:b + 1]], [count_ref[b]])
+        w4 = spread_levels(weights_t(zs[0], halves[0], pulls[0]), levels)
+        if b == 0:
+            keep.wait()
+            for copy in field_copies:
+                copy.wait()
         f = fields[:, :, b * cut:(b + 1) * cut].reshape(rows, cut)
         made[b] = analyse(f, w4, levels).reshape(parts, rows // parts, cut)
         window = pl.ds(pl.multiple_of(me * cols + b * cut, 128), cut)
@@ -253,7 +263,7 @@
             pltpu.VMEM((devices, rows, cols), BF16),
             pltpu.VMEM((devices, blocks, share, width), BF16), pltpu.VMEM((devices, blocks, share, width), BF16),
             pltpu.VMEM((blocks, 8, width), F32), pltpu.VMEM((blocks, devices, rows, cols // blocks), BF16),
-            dma(2), dma(4), dma(4)] + [dma(devices)] * 6 + [dma(blocks, devices)] * 2,
+            dma(2), dma(2 + 2 * CHUNKS), dma(2 + 2 * CHUNKS)] + [dma(devices)] * 6 + [dma(blocks, devices)] * 2,
         compiler_params=pltpu.CompilerParams(collective_id=0, has_side_effects=True, vmem_limit_bytes=50 * 2**20),
         name="analysis",
     )(obs_count[0], own, side, slots, loc_bin[0], flat)

time: 76.3 us -> 75.1 us (0.984)
  Pallas kernels: 71.4 us -> 70.2 us
    pallas_call x1, Pallas kernels: 71.4 us -> 70.2 us  [per_device(): pl.pallas_call(functools.partial(main_kernel, devices, space, levels), ou...]
where the time goes in v4:
time: 75.1 us; the launch traced here: 74.9 us
  Pallas kernels  70.2 us (93%)
  local copies, waits for them, and re-layouts  2.58 us (3%)
  other arithmetic  2.06 us (3%)
    pallas_call x1, Pallas kernels, per_device(): pl.pallas_call(functools.partial(main_kernel, devices, space, levels), ou...  70.2 us

profile of v4, /device:TPU:1, one launch (start us, length us, event | category | flops | bytes accessed | tf_op | source)
XLA Modules:
  0.0 74.9 jit_solution(17194169840681528727)
XLA Ops:
  0.0 0.0 copy-start.3
  0.0 0.0 copy-start.2
  0.0 0.7 copy-done.3
  0.7 0.8 %pad_maximum_fusion.side_ref = f32[128,128]{1,0:T(8,128)S(1)} fusion(f32[64,128]{1,0:T(8,128)} %bitcast.6, f32[64,128]{1,0:T(8,128)} %bitcast.7), kind=kLoop, calls=%fused_computation | loop fusion | flops 16384 | bytes 131072 | tf_op jit(solution)/shard_map/concatenate | solution.py:246
  1.5 1.3 %convert_element_type.3.own_ref = bf16[32,8192]{1,0:T(8,128)(2,1)S(1)} convert(f32[32,8192]{1,0:T(8,128)} %param.8) | non-fusion elementwise | flops 262144 | bytes 1572864 | tf_op jit(solution)/shard_map/convert_element_type | solution.py:245
  2.8 0.0 copy-done.2
  2.8 0.0 copy-start
  2.8 0.0 copy-start.1
  2.8 0.3 reshape.18.field_ref
  3.1 0.4 copy-done
  3.5 0.0 copy-done.1
  3.5 70.2 %analysis.1 = bf16[128,4096]{1,0:T(8,128)(2,1)S(1)} custom-call(s32[2]{0:T(128)S(1)} %bitcast.5, bf16[32,8192]{1,0:T(8,128)(2,1)S(1)} %convert_element_type.3.own_ref, f32[128,128]{1,0:T(8,128)S(1)} %pad_maximum_fusion.side_ref, s32[8,128]{1,0:T(8,128)S(1)} %reshape.17.slot_ref, s32[2,512]{1,0:T(2,128)S(1)} %bitcast.4, bf16[128,4096]{1,0:T(8,128)(2,1)S(1)} %reshape.18.field_ref), custom_call_target="tpu_custom_call" | custom-call | tf_op jit(solution)/shard_map/analysis/pallas_call | solution.py:253
  73.7 1.2 %reshape.19 = bf16[32,4,4096]{2,1,0:T(4,128)(2,1)} reshape(bf16[128,4096]{1,0:T(8,128)(2,1)S(1)} %analysis.1) | data formatting | bytes 2097152 | tf_op jit(solution)/shard_map/reshape | solution.py:270
  (1 shorter events, 0.0 us)
Async XLA Ops:
  0.0 0.7 copy-start.3
  0.0 2.8 %copy-start.2 = (bf16[32,4,4096]{2,1,0:T(4,128)(2,1)S(1)}, bf16[32,4,4096]{2,1,0:T(4,128)(2,1)}, u32[]{:S(2)}) copy-start(bf16[32,4,4096]{2,1,0:T(4,128)(2,1)} %param.7) | copy-start | bytes 3145732
  2.8 0.7 copy-start
  2.8 0.7 copy-start.1

commit v5 on v4

--- a/solution.py
+++ b/solution.py
@@ -184,7 +184,7 @@
         halo_copies[2 * c].wait()
         fill(table, before, sbefore, 0, c * piece, piece)
         halo_copies[2 * c + 1].wait()
-        if c == CHUNKS - 1:
+        if c == 0:
             for copy in field_copies:
                 copy.start()
         fill(table, after, safter, 2 * tile_obs, c * piece, piece)

time: 75.1 us -> 70.2 us (0.935)
  Pallas kernels: 70.2 us -> 65.3 us
    pallas_call x1, Pallas kernels: 70.2 us -> 65.3 us  [per_device(): pl.pallas_call(functools.partial(main_kernel, devices, space, levels), ou...]
where the time goes in v5:
time: 70.2 us; the launch traced here: 70 us
  Pallas kernels  65.3 us (93%)
  local copies, waits for them, and re-layouts  2.58 us (4%)
  other arithmetic  2.06 us (3%)
    pallas_call x1, Pallas kernels, per_device(): pl.pallas_call(functools.partial(main_kernel, devices, space, levels), ou...  65.3 us

profile of v5, /device:TPU:1, one launch (start us, length us, event | category | flops | bytes accessed | tf_op | source)
XLA Modules:
  0.0 70.0 jit_solution(3022051348706046669)
XLA Ops:
  0.0 0.0 copy-start.3
  0.0 0.0 copy-start.2
  0.0 0.7 copy-done.3
  0.7 0.8 %pad_maximum_fusion.side_ref = f32[128,128]{1,0:T(8,128)S(1)} fusion(f32[64,128]{1,0:T(8,128)} %bitcast.6, f32[64,128]{1,0:T(8,128)} %bitcast.7), kind=kLoop, calls=%fused_computation | loop fusion | flops 16384 | bytes 131072 | tf_op jit(solution)/shard_map/concatenate | solution.py:246
  1.5 1.3 %convert_element_type.3.own_ref = bf16[32,8192]{1,0:T(8,128)(2,1)S(1)} convert(f32[32,8192]{1,0:T(8,128)} %param.8) | non-fusion elementwise | flops 262144 | bytes 1572864 | tf_op jit(solution)/shard_map/convert_element_type | solution.py:245
  2.8 0.0 copy-done.2
  2.8 0.0 copy-start
  2.8 0.0 copy-start.1
  2.8 0.3 reshape.18.field_ref
  3.1 0.4 copy-done
  3.5 0.0 copy-done.1
  3.5 65.3 %analysis.1 = bf16[128,4096]{1,0:T(8,128)(2,1)S(1)} custom-call(s32[2]{0:T(128)S(1)} %bitcast.5, bf16[32,8192]{1,0:T(8,128)(2,1)S(1)} %convert_element_type.3.own_ref, f32[128,128]{1,0:T(8,128)S(1)} %pad_maximum_fusion.side_ref, s32[8,128]{1,0:T(8,128)S(1)} %reshape.17.slot_ref, s32[2,512]{1,0:T(2,128)S(1)} %bitcast.4, bf16[128,4096]{1,0:T(8,128)(2,1)S(1)} %reshape.18.field_ref), custom_call_target="tpu_custom_call" | custom-call | tf_op jit(solution)/shard_map/analysis/pallas_call | solution.py:253
  68.8 1.2 %reshape.19 = bf16[32,4,4096]{2,1,0:T(4,128)(2,1)} reshape(bf16[128,4096]{1,0:T(8,128)(2,1)S(1)} %analysis.1) | data formatting | bytes 2097152 | tf_op jit(solution)/shard_map/reshape | solution.py:270
  (1 shorter events, 0.0 us)
Async XLA Ops:
  0.0 0.7 copy-start.3
  0.0 2.8 %copy-start.2 = (bf16[32,4,4096]{2,1,0:T(4,128)(2,1)S(1)}, bf16[32,4,4096]{2,1,0:T(4,128)(2,1)}, u32[]{:S(2)}) copy-start(bf16[32,4,4096]{2,1,0:T(4,128)(2,1)} %param.7) | copy-start | bytes 3145732
  2.8 0.7 copy-start
  2.8 0.7 copy-start.1
